TPU v7x, 768 devices: a whole 4x8x12 slice. The times are simulated.
768 devices in a mesh: space: 12 (over z_hi, x), inst: 8 (over y), blade: 8 (over z_lo, core).
Axes of the slice: x: 4, y: 8, z: 12 (z_hi: 3, z_lo: 4; z = z_hi * 4 + z_lo), core: 2. Of those that a mesh axis runs over, the one named last changes fastest.
Arguments:
- state: bfloat16 [8, 16, 5, 96, 1024], P('blade', 'inst', None, 'space'), may hold values from -6 to 6
- flux_x: float32 [5, 5], replicated, may hold values from -2.5 to 2.5
- flux_c: float32 [5, 5], replicated, may hold values from -2.5 to 2.5
- pressure_weights: float32 [5], replicated, may hold values from 0.2 to 1
- coupling: float32 [5], replicated, may hold values from -1.5 to 1.5
- mode_shapes: float32 [8, 64, 3072], P('blade', None, 'space'), may hold values from -6 to 6
- stiffness: float32 [64], replicated, may hold values from 512 to 4096
- surf_index: int32 [8, 3072], P('blade', 'space'), may hold values from 0 to 8191, as said below
- surf_count: int32 [8, 12], P('blade', 'space'), may hold values from 64 to 256, as said below
- blade_of_row: int32 [8, 3072], P('blade', 'space'), may hold values from 0 to 1
- phase_shift: int32 [16], replicated, may hold values from 0 to 15
Outputs:
- residual: float32 [8, 16, 5, 96, 1024], P('blade', 'inst', None, 'space')
Inputs may be any that keep to these rules, and one draw needn't show every extreme that they name: `surf_index`: within one block the surface row slots name distinct cells, numbered 0 to 8191. `surf_count`: some block in every draw has all 256 slots live.
All inputs are finite; a program needn't handle non-finite values.
Results may differ from a plain program's by a relative error of at most 0.0003.
Values may be sent and summed in bfloat16 or wider, within the bound.
A program may use at most 32 MiB of HBM per device.

v0:
```python
import jax
import jax.numpy as jnp
from jax import lax
from jax.sharding import PartitionSpec as P

COMP = 5
CX = 8
NC = 1024
BPG = 2


HIGH = lax.Precision.HIGHEST


def padded_2(cells, sides, width):
    for axis, dim in sides:
        count = lax.axis_size(axis)
        ends = count - 1
        head = lax.slice_in_dim(cells, 0, width, axis=dim)
        tail = lax.slice_in_dim(cells, cells.shape[dim] - width, cells.shape[dim], axis=dim)
        cells = jnp.concatenate(
            [
                lax.ppermute(tail, axis, [(i, (i + 1) % count) for i in range(ends)]),
                cells,
                lax.ppermute(head, axis, [((i + 1) % count, i) for i in range(ends)]),
            ],
            axis=dim,
        )
    return cells


def spectral_matrix(count):
    first = jnp.arange(count, dtype=jnp.int32)[:, None]
    second = jnp.arange(count, dtype=jnp.int32)[None, :]
    offset = first - second
    apart = offset != 0
    angle = jnp.pi * offset.astype(jnp.float32) / count
    parity = jnp.where(offset % 2 == 0, 1.0, -1.0).astype(jnp.float32)
    safe_sin = jnp.where(apart, jnp.sin(angle), 1.0)
    cotan = jnp.where(apart, 0.5 * parity * jnp.cos(angle) / safe_sin, 0.0)
    return cotan


def place_cells(index, values):
    return jnp.zeros((CX * NC,), jnp.float32).at[index].add(values)


def body(
    state,
    flux_x,
    flux_c,
    pressure_weights,
    coupling,
    mode_shapes,
    stiffness,
    surf_index,
    surf_count,
    blade_of_row,
    phase_shift,
):
    local = state[0]
    held = local.shape[0]
    ninst = lax.axis_size("inst") * held
    my_inst = lax.axis_index("inst")
    my_group = lax.axis_index("blade")
    qmat = spectral_matrix(ninst)
    padded = padded_2(local, (("space", 2),), 1).astype(jnp.float32)
    xplus = padded[:, :, 2:, :]
    xminus = padded[:, :, :-2, :]
    u = padded[:, :, 1:-1, :]
    cplus = jnp.roll(u, -1, axis=3)
    cminus = jnp.roll(u, 1, axis=3)
    flow_x = jnp.einsum("kc,icxw->ikxw", flux_x, xplus - xminus, precision=HIGH)
    flow_c = jnp.einsum("kc,icxw->ikxw", flux_c, cplus - cminus, precision=HIGH)
    space = 0.5 * flow_x + 0.5 * flow_c - 0.25 * (xplus + xminus + cplus + cminus - 4.0 * u)
    first_inst = my_inst * held
    my_rows = lax.dynamic_slice_in_dim(qmat, first_inst, held, 0)
    spect = jnp.einsum(
        "ij,jcxw->icxw",
        my_rows,
        lax.all_gather(local, "inst", axis=0, tiled=True).astype(jnp.float32),
        precision=HIGH,
    )
    cells = CX * NC
    index = surf_index[0]
    count = surf_count[0, 0]
    owner = blade_of_row[0]
    phi = mode_shapes[0]
    pfield = jnp.einsum("k,ikn->in", pressure_weights, u.reshape(held, COMP, cells), precision=HIGH)
    prow = pfield[:, index]
    live = jnp.arange(index.shape[0], dtype=jnp.int32) < count
    onehot = ((owner[:, None] == jnp.arange(BPG, dtype=jnp.int32)[None, :]) & live[:, None]).astype(
        jnp.float32
    )
    force = jnp.einsum("mr,ir,rq->imq", phi, prow, onehot, precision=HIGH)
    shifts = lax.dynamic_slice_in_dim(phase_shift, my_group * BPG, BPG)
    instances = first_inst + jnp.arange(held, dtype=jnp.int32)
    column = (instances[:, None] - shifts[None, :]) % ninst
    select = (column[..., None] == jnp.arange(ninst, dtype=jnp.int32)).astype(jnp.float32)
    placed = jnp.einsum("imq,iqt->mt", force, select, precision=HIGH)
    reference_force = lax.psum(placed, ("space", "inst", "blade"))
    amplitude = reference_force / stiffness[:, None]
    blade_amp = jnp.einsum("mt,iqt->imq", amplitude, select, precision=HIGH)
    displacement = jnp.einsum("mr,imq,rq->ir", phi, blade_amp, onehot, precision=HIGH)
    dfield = jax.vmap(place_cells, (None, 0))(index, displacement).reshape(held, CX, NC)
    total = spect + space + coupling[None, :, None, None] * dfield[:, None, :, :]
    return total[None]


def solution(mesh):
    placed = (
        P("blade", "inst", None, "space", None),
        P(),
        P(),
        P(),
        P(),
        P("blade", None, "space"),
        P(),
        P("blade", "space"),
        P("blade", "space"),
        P("blade", "space"),
        P(),
    )
    return jax.shard_map(
        body,
        mesh=mesh,
        in_specs=placed,
        out_specs=P("blade", "inst", None, "space", None),
        check_vma=False,
    )
```

profile of v0, /device:TPU:1, one launch (start us, length us, event | category | flops | bytes accessed | tf_op | source)
XLA Modules:
  0.0 169.1 jit_solution(17164559572315220966)
XLA Ops:
  6.6 1.1 fusion.59
  7.7 3.9 %collective-permute-start = (bf16[2,5,1,1024]{3,2,1,0:T(2,128)(2,1)S(1)}, bf16[2,5,1,1024]{3,2,1,0:T(2,128)(2,1)S(1)}, u32[]{:S(2)}, u32[]{:S(2)}) collective-permute-start(bf16[2,5,1,1024]{3,2,1,0:T(2,128)(2,1)S(1)} %get-tuple-element.9), channel_id=1, source_target_pairs={{0,64},{64,128},{128,192},{192,256},{256,320},{320,384},{384,448},... | collective-permute-start | bytes 61448 | tf_op jit(solution)/shard_map/ppermute | solution.py:23
  11.6 1.3 collective-permute-start.1
  12.9 1.1 reshape.109
  14.1 0.7 compare_select_fusion
  14.8 1.0 fusion.50
  15.8 2.6 %copy.56 = f32[1,2,8192]{1,2,0:T(8,128)} copy(f32[1,2,8192]{2,0,1:T(1,128)S(1)} %fusion.50) | data formatting | bytes 131072 | tf_op jit(solution)/shard_map/k,ikn->in/dot_general | solution.py:89
  18.4 2.9 %gather_fusion = f32[256,2]{1,0:T(8,128)S(1)} fusion(f32[2,8192]{0,1:T(8,128)} %bitcast.62, s32[1024]{0:T(1024)S(1)} %pad_clamp_fusion), kind=kCustom, calls=%fused_computation | custom fusion | bytes 5120 | tf_op jit(solution)/shard_map/gather | solution.py:90
  22.3 0.2 convolution_bitcast_fusion.2
  22.5 0.2 convolution_bitcast_fusion
  22.7 126.3 %psum.7 = f32[64,16]{0,1:T(8,128)S(1)} all-reduce(f32[64,16]{0,1:T(8,128)S(1)} %convolution_bitcast_fusion), channel_id=1, replica_groups=mesh['space'=12,'inst'=8,'blade'=8] {'space','inst','blade'}, use_global_device_ids=true, to_apply=%region_0.1 | all-reduce | flops 1024 | bytes 8192 | tf_op jit(solution)/shard_map/psum | solution.py:101
  149.0 0.2 convolution_bitcast_fusion.3
  149.2 0.2 fusion.6
  149.4 0.1 copy.62
  149.6 3.6 %scatter_custom_fusion = f32[2,8192]{0,1:T(8,128)} fusion(s32[256]{0:T(256)S(1)} %bitcast.68, f32[256,2]{1,0:T(8,128)S(1)} %copy.62, f32[]{:T(128)} %constant.52.clone.1), kind=kCustom, calls=%fused_computation.2 | custom fusion | flops 512 | bytes 65540 | tf_op jit(solution)/shard_map/vmap()/scatter-add | solution.py:45
  153.2 2.9 %copy.51 = f32[2,8,1024]{2,1,0:T(8,128)S(1)} copy(f32[2,8,1024]{0,2,1:T(8,128)} %bitcast.61) | data formatting | bytes 131072 | tf_op jit(solution)/shard_map/mul | solution.py:106
  156.1 0.1 maximum_convert_fusion.2
  156.2 0.1 maximum_convert_fusion
  156.3 0.2 fusion.58
  156.5 0.2 fusion.18
  156.7 0.7 fusion.7
  157.5 0.7 fusion.9
  158.2 2.6 %fusion.2 = f32[2,5,8,1024]{3,0,2,1:T(2,128)S(1)} fusion(bf16[1,16,5,8,1024]{4,3,2,0,1:T(8,128)(2,1)} %all-gather.3.cloned.1.call-done, s32[16,16]{1,0:T(8,128)S(1)} %get-tuple-element.11, s32[]{:T(128)S(6)} %select_n.49, s32[16,16]{1,0:T(8,128)S(1)} %get-tuple-element.12), kind=kOutput, calls=%fused_computation.4 | convolution fusion | flops 15728960 | bytes 1640452 | tf_op jit(solution)/shard_map/ij,jcxw->icxw/dot_general | solution.py:78
  160.8 1.4 fusion.16
  (31 shorter events, 0.5 us)
Async XLA Ops:
  6.5 15.8 %copy-start = (f32[1,64,256]{2,1,0:T(8,128)S(1)}, f32[1,64,256]{2,1,0:T(8,128)}, u32[]{:S(2)}) copy-start(f32[1,64,256]{2,1,0:T(8,128)} %param.16) | copy-start | bytes 196612
  6.5 15.5 %copy-start.6 = (s32[16]{0:T(128)S(1)}, s32[16]{0:T(128)}, u32[]{:S(2)}) copy-start(s32[16]{0:T(128)} %param.21) | copy-start | bytes 196
  6.5 15.7 %copy-start.4 = (s32[1,256]{1,0:T(1,128)S(1)}, s32[1,256]{1,0:T(1,128)}, u32[]{:S(2)}) copy-start(s32[1,256]{1,0:T(1,128)} %param.20) | copy-start | bytes 3076
  6.5 142.5 %copy-start.7 = (f32[64]{0:T(128)S(1)}, f32[64]{0:T(128)}, u32[]{:S(2)}) copy-start(f32[64]{0:T(128)} %param.17) | copy-start | bytes 772
  6.5 151.7 %all-gather.3.cloned.1.call-start = ((), (), s32[]{:S(2)}) async-start(), calls=%async_computation | async-start | bytes 1474560 | tf_op jit(solution)/shard_map/all_gather | solution.py:81
  7.7 148.4 %collective-permute-start = (bf16[2,5,1,1024]{3,2,1,0:T(2,128)(2,1)S(1)}, bf16[2,5,1,1024]{3,2,1,0:T(2,128)(2,1)S(1)}, u32[]{:S(2)}, u32[]{:S(2)}) collective-permute-start(bf16[2,5,1,1024]{3,2,1,0:T(2,128)(2,1)S(1)} %get-tuple-element.9), channel_id=1, source_target_pairs={{0,64},{64,128},{128,192},{192,256},{256,320},{320,384},{384,448},... | collective-permute-start | bytes 61448 | tf_op jit(solution)/shard_map/ppermute | solution.py:23
  11.6 144.4 %collective-permute-start.1 = (bf16[2,5,1,1024]{3,2,1,0:T(2,128)(2,1)S(1)}, bf16[2,5,1,1024]{3,2,1,0:T(2,128)(2,1)S(1)}, u32[]{:S(2)}, u32[]{:S(2)}) collective-permute-start(bf16[2,5,1,1024]{3,2,1,0:T(2,128)(2,1)S(1)} %get-tuple-element.10), channel_id=1, source_target_pairs={{64,0},{128,64},{192,128},{256,192},{320,256},{384,320},{448,384},... | collective-permute-start | bytes 61448 | tf_op jit(solution)/shard_map/ppermute | solution.py:25
  149.6 6.5 %copy-start.1 = (bf16[1,2,5,8,1024]{4,3,2,1,0:T(8,128)(2,1)S(1)}, bf16[1,2,5,8,1024]{4,3,2,1,0:T(8,128)(2,1)}, u32[]{:S(2)}) copy-start(bf16[1,2,5,8,1024]{4,3,2,1,0:T(8,128)(2,1)} %param.11) | copy-start | bytes 491524
  153.1 3.6 %copy-start.2 = (f32[5,5]{1,0:T(8,128)S(1)}, f32[5,5]{1,0:T(8,128)}, u32[]{:S(2)}) copy-start(f32[5,5]{1,0:T(8,128)} %param.13) | copy-start | bytes 304
  153.1 4.3 %copy-start.3 = (f32[5,5]{1,0:T(8,128)S(1)}, f32[5,5]{1,0:T(8,128)}, u32[]{:S(2)}) copy-start(f32[5,5]{1,0:T(8,128)} %param.12) | copy-start | bytes 304
  156.0 4.8 %copy-start.5 = (f32[5]{0:T(128)S(1)}, f32[5]{0:T(128)}, u32[]{:S(2)}) copy-start(f32[5]{0:T(128)} %param.15) | copy-start | bytes 64
Sparse Core Ops, SparseCore 0:
  13.1 52.1 all-gather.2
where the time goes:
time: 169 us
  blocking collectives  126 us (75%)
  between operations  14.3 us (8%)
  local copies, waits for them, and re-layouts  11.1 us (7%)
  other arithmetic  6.33 us (4%)
  matrix products  5.83 us (3%)
  starting transfers between devices  5.27 us (3%)
    psum x1, blocking collectives, body(): reference_force = lax.psum(placed, ('space', 'inst', 'blade'))  126 us
    ppermute x1, starting transfers between devices, padded_2(): lax.ppermute(tail, axis, [(i, (i + 1) % count) for i in range(ends)])  3.95 us
    scatter-add x1, other arithmetic, place_cells(): return jnp.zeros((CX * NC,), jnp.float32).at[index].add(values)  3.58 us
  transfers between devices with their start and end apart: 3, of which 0 were waited for; matrix products, arithmetic and copies ran while one was open for 11% of the time, Pallas kernels for 0%

commit v1 on v0

v1 whole, which is shorter than its diff:
```python
import functools
import math

import jax
import jax.numpy as jnp
from jax import lax
from jax.experimental import pallas as pl
from jax.experimental.pallas import tpu as pltpu
from jax.sharding import PartitionSpec as P

COMP = 5
CX = 8
NC = 1024
MODES = 64
ROWS = 256
BPG = 2
HELD = 2
PLANES = HELD * COMP
DEEP = PLANES * CX
LANES = 128
NB_LANE = NC // LANES
CHUNKS = 4
WIDTH = NC // CHUNKS

HIGH = lax.Precision.HIGHEST
MESH = pl.DeviceIdType.MESH
F32 = jnp.float32


def spectral(offset, count):
    offset %= count
    if offset == 0:
        return 0.0
    angle = math.pi * offset / count
    return 0.5 * (-1.0) ** offset * math.cos(angle) / math.sin(angle)


def dot(a, b, dims):
    return lax.dot_general(a, b, (dims, ((), ())), precision=HIGH, preferred_element_type=F32)


def kernel(
    sizes,
    state,
    fx,
    fc,
    pw,
    cpl,
    modes,
    stiff,
    index,
    count,
    owner,
    shift,
    out,
    mine,
    phi,
    dcs,
    fromleft,
    fromright,
    hrow,
    hsend,
    hrecv,
    pf,
    dsc,
    part,
    box0,
    box1,
    box2,
    load_sem,
    sl_sem,
    rl_sem,
    sr_sem,
    rr_sem,
    hs_sem,
    hr_sem,
    as_sem,
    ar_sem,
):
    n_space, n_inst, n_blade = sizes
    half = n_inst // 2
    ninst = n_inst * HELD
    my_space = lax.axis_index("space")
    my_inst = lax.axis_index("inst")
    my_blade = lax.axis_index("blade")

    loads = [
        pltpu.make_async_copy(state, mine, load_sem.at[0]),
        pltpu.make_async_copy(modes, phi.at[pl.ds(0, MODES)], load_sem.at[1]),
        pltpu.make_async_copy(modes, phi.at[pl.ds(MODES, MODES)], load_sem.at[2]),
    ]
    for copy in loads:
        copy.start()

    stages = (("space", n_space, my_space, box0), ("blade", n_blade, my_blade, box1), ("inst", n_inst, my_inst, box2))
    barrier = pltpu.get_barrier_semaphore()
    for axis, size, me, _ in stages:
        for k in range(1, size):
            pl.semaphore_signal(barrier, inc=1, device_id={axis: lax.rem(me + k, size)}, device_id_type=MESH)
    pl.semaphore_wait(barrier, n_space + n_inst + n_blade - 3)

    right = lax.rem(my_inst + 1, n_inst)
    left = lax.rem(my_inst + n_inst - 1, n_inst)

    def columns(chunk):
        return pl.ds(chunk * WIDTH, WIDTH)

    def to_right(hop, chunk):
        src = mine if hop == 1 else fromleft.at[hop - 2]
        return pltpu.make_async_remote_copy(
            src_ref=src.at[:, columns(chunk)],
            dst_ref=fromleft.at[hop - 1, :, columns(chunk)],
            send_sem=sr_sem.at[hop - 1, chunk],
            recv_sem=rl_sem.at[hop - 1, chunk],
            device_id={"inst": right},
            device_id_type=MESH,
        )

    def to_left(hop, chunk):
        src = mine if hop == 1 else fromright.at[hop - 2]
        return pltpu.make_async_remote_copy(
            src_ref=src.at[:, columns(chunk)],
            dst_ref=fromright.at[hop - 1, :, columns(chunk)],
            send_sem=sl_sem.at[hop - 1, chunk],
            recv_sem=rr_sem.at[hop - 1, chunk],
            device_id={"inst": left},
            device_id_type=MESH,
        )

    def going(hop):
        rights = [c for c in range(CHUNKS) if hop < half or c < CHUNKS // 2]
        lefts = [c for c in reversed(range(CHUNKS)) if hop < half or c >= CHUNKS // 2]
        return list(zip(rights, lefts))

    loads[0].wait()
    for c_right, c_left in going(1):
        to_right(1, c_right).start()
        to_left(1, c_left).start()

    def block(ref, lanes):
        got = []
        for group in range(DEEP // 16):
            pair = ref[pl.ds(16 * group, 16), lanes].astype(F32)
            got += [pair[0:CX], pair[CX : 2 * CX]]
        return got

    def lane_block(j):
        return pl.ds(pl.multiple_of(j * LANES, LANES), LANES)

    def pressure(j, carry):
        planes = block(mine, lane_block(j))
        for i in range(HELD):
            total = pw[0] * planes[i * COMP]
            for k in range(1, COMP):
                total = total + pw[k] * planes[i * COMP + k]
            pf[pl.ds(pl.multiple_of(j * CX, CX), CX), pl.ds(i * LANES, LANES)] = total
        return carry

    lax.fori_loop(0, NB_LANE, pressure, 0)

    cell = index[...]
    high = ((cell >> 7) & 7) * CX + (cell >> 10)
    low = cell & (LANES - 1)
    at_high = (lax.broadcasted_iota(jnp.int32, (CX * NB_LANE, ROWS), 0) == high).astype(F32)
    at_low = lax.broadcasted_iota(jnp.int32, (LANES, ROWS), 0) == low
    live = lax.broadcasted_iota(jnp.int32, (1, ROWS), 1) < count[0, 0]
    lag = jnp.where(owner[...] == 0, shift[my_blade * BPG], shift[my_blade * BPG + 1])
    slot = lax.broadcasted_iota(jnp.int32, (ninst, ROWS), 0)
    picks = [(((my_inst * HELD + i - lag) & (ninst - 1)) == slot) & live for i in range(HELD)]

    rows = dot(pf[...], at_high, ((0,), (0,)))
    placed = jnp.zeros((ninst, ROWS), F32)
    for i in range(HELD):
        prow = jnp.sum(jnp.where(at_low, rows[i * LANES : (i + 1) * LANES], 0.0), axis=0, keepdims=True)
        placed = placed + jnp.where(picks[i], prow, 0.0)
    loads[1].wait()
    loads[2].wait()
    force = dot(placed, phi[...], ((1,), (1,)))
    first_half = lax.broadcasted_iota(jnp.int32, (CX, LANES), 1) < MODES
    part[0] = jnp.where(first_half, force[0:CX], force[CX : 2 * CX])

    def send_part(s):
        axis, size, me, box = stages[s]
        for k in range(1, size):
            pltpu.make_async_remote_copy(
                src_ref=part.at[s],
                dst_ref=box.at[k - 1],
                send_sem=as_sem.at[s],
                recv_sem=ar_sem.at[s],
                device_id={axis: lax.rem(me + k, size)},
                device_id_type=MESH,
            ).start()

    def sum_part(s):
        size, box = stages[s][1], stages[s][3]
        pltpu.make_async_copy(box, box, ar_sem.at[s]).wait()
        total = part[s]
        for k in range(size - 1):
            total = total + box[k]
        return total

    send_part(0)

    hrow[...] = jnp.zeros_like(hrow)
    for group in range(DEEP // 16):
        pair = mine[pl.ds(16 * group, 16), :].astype(F32)
        for odd in range(2):
            plane = 2 * group + odd
            hrow[0, pl.ds(plane, 1), :] = pair[odd * CX : odd * CX + 1]
            hrow[1, pl.ds(plane, 1), :] = pair[odd * CX + CX - 1 : odd * CX + CX]
    for side in range(2):
        hsend[side] = hrow[side].astype(jnp.bfloat16)
    halos = []
    for side, step in ((0, n_space - 1), (1, 1)):
        halos.append(
            pltpu.make_async_remote_copy(
                src_ref=hsend.at[side],
                dst_ref=hrecv.at[side],
                send_sem=hs_sem.at[side],
                recv_sem=hr_sem.at[side],
                device_id={"space": lax.rem(my_space + step, n_space)},
                device_id_type=MESH,
            )
        )
        halos[-1].start()

    for group in range(DEEP // 16):
        pair = mine[pl.ds(16 * group, 16), :].astype(F32)
        ahead = pltpu.roll(pair, NC - 1, 1)
        behind = pltpu.roll(pair, 1, 1)
        dcs[pl.ds(16 * group, 16), :] = ahead - behind
        out[pl.ds(16 * group, 16), :] = pair - 0.25 * (ahead + behind)

    for copy in halos:
        copy.wait_recv()
    nexts = hrecv[0].astype(F32) * jnp.where(my_space == n_space - 1, 0.0, 1.0)
    hrow[0] = nexts
    hrow[1] = hrecv[1].astype(F32) * jnp.where(my_space == 0, 0.0, 1.0)

    layer = lax.broadcasted_iota(jnp.int32, (CX, LANES), 0)

    def local(j, carry):
        lanes = lane_block(j)
        planes = block(mine, lanes)
        for i in range(HELD):
            dx, dc = [], []
            for k in range(COMP):
                p = i * COMP + k
                up = jnp.where(layer == CX - 1, hrow[0, pl.ds(p, 1), lanes], pltpu.roll(planes[p], CX - 1, 0))
                down = jnp.where(layer == 0, hrow[1, pl.ds(p, 1), lanes], pltpu.roll(planes[p], 1, 0))
                dx.append(up - down)
                dc.append(dcs[pl.ds(p * CX, CX), lanes])
                at = pl.ds(p * CX, CX)
                value = out[at, lanes] - 0.25 * (up + down)
                for r in range(HELD):
                    value = value + spectral(i - r, ninst) * planes[r * COMP + k]
                out[at, lanes] = value
            for k in range(COMP):
                at = pl.ds((i * COMP + k) * CX, CX)
                flow = fx[k, 0] * dx[0] + fc[k, 0] * dc[0]
                for c in range(1, COMP):
                    flow = flow + fx[k, c] * dx[c] + fc[k, c] * dc[c]
                out[at, lanes] = out[at, lanes] + 0.5 * flow
        return carry

    lax.fori_loop(0, NB_LANE, local, 0)

    def add_blocks(sources, first, last):
        def add(j, carry):
            lanes = lane_block(j)
            sums = [out[pl.ds(p * CX, CX), lanes] for p in range(PLANES)]
            for ref, offset in sources:
                planes = block(ref, lanes)
                for i in range(HELD):
                    for k in range(COMP):
                        for r in range(HELD):
                            sums[i * COMP + k] += spectral(HELD * offset + i - r, ninst) * planes[r * COMP + k]
            for p in range(PLANES):
                out[pl.ds(p * CX, CX), lanes] = sums[p]
            return carry

        lax.fori_loop(first, last, add, 0)

    for hop in range(1, half + 1):
        onward = going(hop + 1) if hop < half else []
        for pair in going(hop):
            to_right(hop, pair[0]).wait_recv()
            if pair[0] in [c for c, _ in onward]:
                to_right(hop + 1, pair[0]).start()
            to_left(hop, pair[1]).wait_recv()
            if pair[1] in [c for _, c in onward]:
                to_left(hop + 1, pair[1]).start()
        if hop == 1:
            part[1] = sum_part(0)
            send_part(1)
        if hop == 2:
            part[2] = sum_part(1)
            send_part(2)
        if hop == 3:
            total = sum_part(2)
            rigid = jnp.concatenate([stiff[...], stiff[...]], axis=1)
            amp = total / rigid
            both = jnp.concatenate([jnp.where(first_half, amp, 0.0), jnp.where(first_half, 0.0, amp)], axis=0)
            moved = dot(both, phi[...], ((1,), (0,)))
            spread = []
            for i in range(HELD):
                disp = jnp.sum(jnp.where(picks[i], moved, 0.0), axis=0, keepdims=True)
                spread.append(jnp.where(at_low, disp, 0.0))
            dsc[...] = dot(at_high, jnp.concatenate(spread, axis=0), ((1,), (1,)))

            def wall(j, carry):
                lanes = lane_block(j)
                for i in range(HELD):
                    field = dsc[pl.ds(pl.multiple_of(j * CX, CX), CX), pl.ds(i * LANES, LANES)]
                    for k in range(COMP):
                        at = pl.ds((i * COMP + k) * CX, CX)
                        out[at, lanes] = out[at, lanes] + cpl[k] * field
                return carry

            lax.fori_loop(0, NB_LANE, wall, 0)
        if hop < half:
            add_blocks([(fromleft.at[hop - 1], hop), (fromright.at[hop - 1], -hop)], 0, NB_LANE)
        else:
            add_blocks([(fromleft.at[hop - 1], hop)], 0, NB_LANE // 2)
            add_blocks([(fromright.at[hop - 1], -hop)], NB_LANE // 2, NB_LANE)

    for hop in range(1, half + 1):
        for c_right, c_left in going(hop):
            to_right(hop, c_right).wait_send()
            to_left(hop, c_left).wait_send()
    for copy in halos:
        copy.wait_send()
    for s in range(3):
        box = stages[s][3]
        pltpu.make_async_copy(box, box, as_sem.at[s]).wait()


def body(sizes, state, fx, fc, pw, cpl, modes, stiff, index, count, owner, shift):
    n_space, n_inst, n_blade = sizes
    half = n_inst // 2
    smem = pl.BlockSpec(memory_space=pltpu.SMEM)
    vmem = pl.BlockSpec(memory_space=pltpu.VMEM)
    hbm = pl.BlockSpec(memory_space=pl.ANY)
    dma = pltpu.SemaphoreType.DMA
    out = pl.pallas_call(
        functools.partial(kernel, sizes),
        out_shape=jax.ShapeDtypeStruct((DEEP, NC), F32),
        in_specs=[hbm, smem, smem, smem, smem, hbm, vmem, vmem, smem, vmem, smem],
        out_specs=vmem,
        scratch_shapes=[
            pltpu.VMEM((DEEP, NC), jnp.bfloat16),
            pltpu.VMEM((2 * MODES, ROWS), F32),
            pltpu.VMEM((DEEP, NC), F32),
            pltpu.VMEM((half, DEEP, NC), jnp.bfloat16),
            pltpu.VMEM((half, DEEP, NC), jnp.bfloat16),
            pltpu.VMEM((2, 16, NC), F32),
            pltpu.VMEM((2, 16, NC), jnp.bfloat16),
            pltpu.VMEM((2, 16, NC), jnp.bfloat16),
            pltpu.VMEM((CX * NB_LANE, HELD * LANES), F32),
            pltpu.VMEM((CX * NB_LANE, HELD * LANES), F32),
            pltpu.VMEM((3, CX, LANES), F32),
            pltpu.VMEM((n_space - 1, CX, LANES), F32),
            pltpu.VMEM((n_blade - 1, CX, LANES), F32),
            pltpu.VMEM((n_inst - 1, CX, LANES), F32),
            dma((3,)),
            dma((half, CHUNKS)),
            dma((half, CHUNKS)),
            dma((half, CHUNKS)),
            dma((half, CHUNKS)),
            dma((2,)),
            dma((2,)),
            dma((3,)),
            dma((3,)),
        ],
        compiler_params=pltpu.CompilerParams(
            collective_id=0, has_side_effects=True, vmem_limit_bytes=24 * 1024 * 1024
        ),
        name="residual",
    )(
        state.reshape(DEEP, NC),
        fx,
        fc,
        pw,
        cpl,
        modes.reshape(MODES, ROWS),
        stiff.reshape(1, MODES),
        index,
        count,
        owner,
        shift,
    )
    return out.reshape(1, HELD, COMP, CX, NC)


def solution(mesh):
    sizes = (mesh.shape["space"], mesh.shape["inst"], mesh.shape["blade"])
    placed = (
        P("blade", "inst", None, "space", None),
        P(),
        P(),
        P(),
        P(),
        P("blade", None, "space"),
        P(),
        P("blade", "space"),
        P("blade", "space"),
        P("blade", "space"),
        P(),
    )
    return jax.shard_map(
        functools.partial(body, sizes),
        mesh=mesh,
        in_specs=placed,
        out_specs=P("blade", "inst", None, "space", None),
        check_vma=False,
    )
```

time: 169 us -> 45.5 us (0.27)
  blocking collectives: 126 us -> 0 us
  Pallas kernels: 0 us -> 40 us
  between operations: 14.3 us -> 0.73 us
  local copies, waits for them, and re-layouts: 11.1 us -> 4.5 us
  other arithmetic: 6.33 us -> 0 us
  matrix products: 5.83 us -> 0 us
  starting transfers between devices: 5.27 us -> 0 us
    psum x1 -> x0, blocking collectives: 126 us -> none  [body(): reference_force = lax.psum(placed, ('space', 'inst', 'blade'))]
    pallas_call x0 -> x1, Pallas kernels: none -> 40 us  [body(): pl.pallas_call(functools.partial(kernel, sizes), out_shape=jax.ShapeDtype...]
    dot_general x8 -> x0, matrix products: 5.83 us -> none  [the longest x1 2.58 us: body(): jnp.einsum('ij,jcxw->icxw', my_rows, lax.all_gather(local, 'inst', axis=0...]
    ppermute x2 -> x0, starting transfers between devices: 5.24 us -> none  [the longest x1 3.95 us: padded_2(): lax.ppermute(tail, axis, [(i, (i + 1) % count) for i in range(ends)])]
    unnamed x16 -> x21, local copies, waits for them, and re-layouts: 0.04 us -> 4.5 us
    scatter-add x1 -> x0, other arithmetic: 3.58 us -> none  [place_cells(): return jnp.zeros((CX * NC,), jnp.float32).at[index].add(values)]
    gather x2 -> x0, local copies, waits for them, and re-layouts: 2.98 us -> none  [body(): prow = pfield[:, index]]
    mul x1 -> x0, local copies, waits for them, and re-layouts: 2.87 us -> none  [body(): coupling[None, :, None, None] * dfield[:, None, :, :]]
  transfers between devices with their start and end apart: 3 -> 0, of which waited for: 0 -> 0; matrix products, arithmetic and copies ran while one was open for 11% -> 0% of each run, Pallas kernels for 0% -> 0%
where the time goes in v1:
time: 45.5 us; the launch traced here: 45.2 us
  Pallas kernels  40 us (88%)
  local copies, waits for them, and re-layouts  4.5 us (10%)
  between operations  0.73 us (2%)
    pallas_call x1, Pallas kernels, body(): pl.pallas_call(functools.partial(kernel, sizes), out_shape=jax.ShapeDtype...  40 us
    unnamed x21, local copies, waits for them, and re-layouts  4.5 us

profile of v1, /device:TPU:1, one launch (start us, length us, event | category | flops | bytes accessed | tf_op | source)
XLA Modules:
  0.0 45.2 jit_solution(15710012387609008672)
XLA Ops:
  0.0 0.0 copy-start.2
  0.7 0.0 copy-start.5
  0.7 0.0 copy-start.7
  0.7 0.0 copy-start.8
  0.7 0.0 copy-start.4
  0.7 0.0 copy-start.6
  0.7 0.0 copy-done.2
  0.7 0.6 %copy-done.5 = s32[1,256]{1,0:T(1,128)S(1)} copy-done((s32[1,256]{1,0:T(1,128)S(1)}, s32[1,256]{1,0:T(1,128)}, u32[]{:S(2)}) %copy-start.5) | copy-done | bytes 1048
  1.3 0.0 copy-done.7
  1.4 0.0 copy-done.8
  1.4 0.0 copy-done.4
  1.4 0.0 copy-done.6
  1.4 0.0 copy-start
  1.4 0.9 %copy-done = bf16[1,2,5,8,1024]{4,3,2,1,0:T(8,128)(2,1)S(1)} copy-done((bf16[1,2,5,8,1024]{4,3,2,1,0:T(8,128)(2,1)S(1)}, bf16[1,2,5,8,1024]{4,3,2,1,0:T(8,128)(2,1)}, u32[]{:S(2)}) %copy-start) | copy-done | bytes 163864
  2.3 0.0 copy-start.1
  2.3 0.8 %copy-done.1 = f32[1,64,256]{2,1,0:T(8,128)S(1)} copy-done((f32[1,64,256]{2,1,0:T(8,128)S(1)}, f32[1,64,256]{2,1,0:T(8,128)}, u32[]{:S(2)}) %copy-start.1) | copy-done | bytes 65560
  3.2 0.0 copy-start.3
  3.2 0.7 %copy-done.3 = f32[5,5]{1,0:T(8,128)S(1)} copy-done((f32[5,5]{1,0:T(8,128)S(1)}, f32[5,5]{1,0:T(8,128)}, u32[]{:S(2)}) %copy-start.3) | copy-done | bytes 124
  3.8 0.0 copy-start.9
  3.8 0.7 %copy-done.9 = s32[16]{0:T(128)S(1)} copy-done((s32[16]{0:T(128)S(1)}, s32[16]{0:T(128)}, u32[]{:S(2)}) %copy-start.9) | copy-done | bytes 88
  4.5 40.0 %residual.1 = f32[80,1024]{1,0:T(8,128)S(1)} custom-call(bf16[80,1024]{1,0:T(8,128)(2,1)S(1)} %bitcast.5, f32[5,5]{1,0:T(8,128)S(1)} %copy-done.2, f32[5,5]{1,0:T(8,128)S(1)} %copy-done.3, f32[5]{0:T(128)S(1)} %copy-done.6, f32[5]{0:T(128)S(1)} %copy-done.7, f32[64,256]{1,0:T(8,128)S(1)} %bitcast.6, f32[1,64]{1,0:T(1,128)S(1)} %bitcast.7, ...), custom_call_target="tpu_custom_call" | custom-call | tf_op jit(solution)/shard_map/residual/pallas_call | solution.py:345
  44.5 0.7 %copy.14 = f32[1,2,5,8,1024]{4,3,2,1,0:T(8,128)} copy(f32[1,2,5,8,1024]{4,3,2,1,0:T(8,128)S(1)} %bitcast.4) | data formatting | bytes 655360
Async XLA Ops:
  0.0 0.7 %copy-start.2 = (f32[5,5]{1,0:T(8,128)S(1)}, f32[5,5]{1,0:T(8,128)}, u32[]{:S(2)}) copy-start(f32[5,5]{1,0:T(8,128)} %fx.1) | copy-start | bytes 304
  0.7 0.7 %copy-start.5 = (s32[1,256]{1,0:T(1,128)S(1)}, s32[1,256]{1,0:T(1,128)}, u32[]{:S(2)}) copy-start(s32[1,256]{1,0:T(1,128)} %owner.1) | copy-start | bytes 3076
  0.7 0.7 %copy-start.7 = (f32[5]{0:T(128)S(1)}, f32[5]{0:T(128)}, u32[]{:S(2)}) copy-start(f32[5]{0:T(128)} %cpl.1) | copy-start | bytes 64
  0.7 0.7 %copy-start.8 = (f32[64]{0:T(128)S(1)}, f32[64]{0:T(128)}, u32[]{:S(2)}) copy-start(f32[64]{0:T(128)} %param.17) | copy-start | bytes 772
  0.7 0.7 %copy-start.4 = (s32[1,256]{1,0:T(1,128)S(1)}, s32[1,256]{1,0:T(1,128)}, u32[]{:S(2)}) copy-start(s32[1,256]{1,0:T(1,128)} %index.1) | copy-start | bytes 3076
  0.7 0.7 %copy-start.6 = (f32[5]{0:T(128)S(1)}, f32[5]{0:T(128)}, u32[]{:S(2)}) copy-start(f32[5]{0:T(128)} %pw.1) | copy-start | bytes 64
  1.4 0.9 %copy-start = (bf16[1,2,5,8,1024]{4,3,2,1,0:T(8,128)(2,1)S(1)}, bf16[1,2,5,8,1024]{4,3,2,1,0:T(8,128)(2,1)}, u32[]{:S(2)}) copy-start(bf16[1,2,5,8,1024]{4,3,2,1,0:T(8,128)(2,1)} %param.11) | copy-start | bytes 491524
  2.3 0.8 %copy-start.1 = (f32[1,64,256]{2,1,0:T(8,128)S(1)}, f32[1,64,256]{2,1,0:T(8,128)}, u32[]{:S(2)}) copy-start(f32[1,64,256]{2,1,0:T(8,128)} %param.16) | copy-start | bytes 196612
  3.2 0.7 %copy-start.3 = (f32[5,5]{1,0:T(8,128)S(1)}, f32[5,5]{1,0:T(8,128)}, u32[]{:S(2)}) copy-start(f32[5,5]{1,0:T(8,128)} %fc.1) | copy-start | bytes 304
  3.8 0.7 %copy-start.9 = (s32[16]{0:T(128)S(1)}, s32[16]{0:T(128)}, u32[]{:S(2)}) copy-start(s32[16]{0:T(128)} %shift.1) | copy-start | bytes 196

commit v2 on v1

--- a/solution.py
+++ b/solution.py
@@ -1,4 +1,5 @@
 import functools
+import itertools
 import math
 
 import jax
@@ -21,6 +22,7 @@
 NB_LANE = NC // LANES
 CHUNKS = 4
 WIDTH = NC // CHUNKS
+STAGES = (("x", "y"), ("zhi", "zlo", "core"))
 
 HIGH = lax.Precision.HIGHEST
 MESH = pl.DeviceIdType.MESH
@@ -39,22 +41,69 @@
     return lax.dot_general(a, b, (dims, ((), ())), precision=HIGH, preferred_element_type=F32)
 
 
+SUB = {"zhi": 3, "x": 4, "y": 8, "zlo": 4, "core": 2}
+
+
+def sub_index(at):
+    return {
+        "zhi": at["space"] // SUB["x"],
+        "x": lax.rem(at["space"], SUB["x"]),
+        "y": at["inst"],
+        "zlo": at["blade"] // SUB["core"],
+        "core": lax.rem(at["blade"], SUB["core"]),
+    }
+
+
+def mesh_index(sub):
+    return {
+        "space": sub["zhi"] * SUB["x"] + sub["x"],
+        "inst": sub["y"],
+        "blade": sub["zlo"] * SUB["core"] + sub["core"],
+    }
+
+
+def exchange_stages(sizes):
+    assert sizes == (SUB["zhi"] * SUB["x"], SUB["y"], SUB["zlo"] * SUB["core"])
+
+    def around(offset, size):
+        return min(offset, size - offset)
+
+    def hops(o):
+        return around(o["x"], 4) + around(o["y"], 8) + around((4 * o["zhi"] + o["zlo"]) % 12, 12) + 0.5 * o["core"]
+
+    stages = []
+    for axes in STAGES:
+        ranges = [range(SUB[a]) if a in axes else (0,) for a in SUB]
+        offsets = [dict(zip(SUB, o)) for o in itertools.product(*ranges) if any(o)]
+        stages.append(sorted(offsets, key=lambda o: -hops(o)))
+    return stages
+
+
 def kernel(
     sizes,
-    state,
+    count,
+    state_hbm,
+    fx_hbm,
+    fc_hbm,
+    pw_hbm,
+    cpl_hbm,
+    modes_hbm,
+    stiff_hbm,
+    index_hbm,
+    owner_hbm,
+    shift_hbm,
+    out,
+    field,
+    gain,
+    mine,
+    phi,
     fx,
     fc,
     pw,
-    cpl,
-    modes,
     stiff,
     index,
-    count,
     owner,
     shift,
-    out,
-    mine,
-    phi,
     dcs,
     fromleft,
     fromright,
@@ -62,11 +111,9 @@
     hsend,
     hrecv,
     pf,
-    dsc,
     part,
     box0,
     box1,
-    box2,
     load_sem,
     sl_sem,
     rl_sem,
@@ -84,23 +131,40 @@
     my_inst = lax.axis_index("inst")
     my_blade = lax.axis_index("blade")
 
-    loads = [
-        pltpu.make_async_copy(state, mine, load_sem.at[0]),
-        pltpu.make_async_copy(modes, phi.at[pl.ds(0, MODES)], load_sem.at[1]),
-        pltpu.make_async_copy(modes, phi.at[pl.ds(MODES, MODES)], load_sem.at[2]),
-    ]
+    moves = (
+        (state_hbm, mine),
+        (index_hbm, index),
+        (pw_hbm, pw),
+        (owner_hbm, owner),
+        (shift_hbm, shift),
+        (modes_hbm, phi.at[pl.ds(0, MODES)]),
+        (modes_hbm, phi.at[pl.ds(MODES, MODES)]),
+        (fx_hbm, fx),
+        (fc_hbm, fc),
+        (stiff_hbm, stiff),
+        (cpl_hbm, gain),
+    )
+    loads = [pltpu.make_async_copy(src, dst, load_sem.at[n]) for n, (src, dst) in enumerate(moves)]
     for copy in loads:
         copy.start()
 
-    stages = (("space", n_space, my_space, box0), ("blade", n_blade, my_blade, box1), ("inst", n_inst, my_inst, box2))
-    barrier = pltpu.get_barrier_semaphore()
-    for axis, size, me, _ in stages:
-        for k in range(1, size):
-            pl.semaphore_signal(barrier, inc=1, device_id={axis: lax.rem(me + k, size)}, device_id_type=MESH)
-    pl.semaphore_wait(barrier, n_space + n_inst + n_blade - 3)
+    stages = exchange_stages(sizes)
+    mesh_at = {"space": my_space, "inst": my_inst, "blade": my_blade}
+    my_sub = sub_index(mesh_at)
+
+    def peer(offsets):
+        return mesh_index({a: lax.rem(my_sub[a] + offsets[a], SUB[a]) if offsets[a] else my_sub[a] for a in SUB})
 
     right = lax.rem(my_inst + 1, n_inst)
     left = lax.rem(my_inst + n_inst - 1, n_inst)
+    following = lax.rem(my_space + 1, n_space)
+    preceding = lax.rem(my_space + n_space - 1, n_space)
+
+    barrier = pltpu.get_barrier_semaphore()
+    greeted = [peer(o) for stage in stages for o in stage]
+    greeted += [{"space": following}, {"space": preceding}]
+    for other in greeted:
+        pl.semaphore_signal(barrier, inc=1, device_id=other, device_id_type=MESH)
 
     def columns(chunk):
         return pl.ds(chunk * WIDTH, WIDTH)
@@ -132,11 +196,6 @@
         lefts = [c for c in reversed(range(CHUNKS)) if hop < half or c >= CHUNKS // 2]
         return list(zip(rights, lefts))
 
-    loads[0].wait()
-    for c_right, c_left in going(1):
-        to_right(1, c_right).start()
-        to_left(1, c_left).start()
-
     def block(ref, lanes):
         got = []
         for group in range(DEEP // 16):
@@ -146,6 +205,9 @@
 
     def lane_block(j):
         return pl.ds(pl.multiple_of(j * LANES, LANES), LANES)
+
+    for copy in loads[0:5]:
+        copy.wait()
 
     def pressure(j, carry):
         planes = block(mine, lane_block(j))
@@ -173,33 +235,39 @@
     for i in range(HELD):
         prow = jnp.sum(jnp.where(at_low, rows[i * LANES : (i + 1) * LANES], 0.0), axis=0, keepdims=True)
         placed = placed + jnp.where(picks[i], prow, 0.0)
-    loads[1].wait()
-    loads[2].wait()
+    for copy in loads[5:7]:
+        copy.wait()
     force = dot(placed, phi[...], ((1,), (1,)))
     first_half = lax.broadcasted_iota(jnp.int32, (CX, LANES), 1) < MODES
     part[0] = jnp.where(first_half, force[0:CX], force[CX : 2 * CX])
 
+    boxes = (box0, box1)
+
     def send_part(s):
-        axis, size, me, box = stages[s]
-        for k in range(1, size):
+        for k, offsets in enumerate(stages[s]):
             pltpu.make_async_remote_copy(
                 src_ref=part.at[s],
-                dst_ref=box.at[k - 1],
+                dst_ref=boxes[s].at[k],
                 send_sem=as_sem.at[s],
                 recv_sem=ar_sem.at[s],
-                device_id={axis: lax.rem(me + k, size)},
+                device_id=peer(offsets),
                 device_id_type=MESH,
             ).start()
 
     def sum_part(s):
-        size, box = stages[s][1], stages[s][3]
+        box = boxes[s]
         pltpu.make_async_copy(box, box, ar_sem.at[s]).wait()
         total = part[s]
-        for k in range(size - 1):
+        for k in range(len(stages[s])):
             total = total + box[k]
         return total
 
+    pl.semaphore_wait(barrier, len(greeted))
     send_part(0)
+
+    for c_right, c_left in going(1):
+        to_right(1, c_right).start()
+        to_left(1, c_left).start()
 
     hrow[...] = jnp.zeros_like(hrow)
     for group in range(DEEP // 16):
@@ -211,14 +279,14 @@
     for side in range(2):
         hsend[side] = hrow[side].astype(jnp.bfloat16)
     halos = []
-    for side, step in ((0, n_space - 1), (1, 1)):
+    for side, other in ((0, preceding), (1, following)):
         halos.append(
             pltpu.make_async_remote_copy(
                 src_ref=hsend.at[side],
                 dst_ref=hrecv.at[side],
                 send_sem=hs_sem.at[side],
                 recv_sem=hr_sem.at[side],
-                device_id={"space": lax.rem(my_space + step, n_space)},
+                device_id={"space": other},
                 device_id_type=MESH,
             )
         )
@@ -231,10 +299,14 @@
         dcs[pl.ds(16 * group, 16), :] = ahead - behind
         out[pl.ds(16 * group, 16), :] = pair - 0.25 * (ahead + behind)
 
+    part[1] = sum_part(0)
+    send_part(1)
+
+    for copy in loads[7:]:
+        copy.wait()
     for copy in halos:
         copy.wait_recv()
-    nexts = hrecv[0].astype(F32) * jnp.where(my_space == n_space - 1, 0.0, 1.0)
-    hrow[0] = nexts
+    hrow[0] = hrecv[0].astype(F32) * jnp.where(my_space == n_space - 1, 0.0, 1.0)
     hrow[1] = hrecv[1].astype(F32) * jnp.where(my_space == 0, 0.0, 1.0)
 
     layer = lax.broadcasted_iota(jnp.int32, (CX, LANES), 0)
@@ -263,8 +335,6 @@
                 out[at, lanes] = out[at, lanes] + 0.5 * flow
         return carry
 
-    lax.fori_loop(0, NB_LANE, local, 0)
-
     def add_blocks(sources, first, last):
         def add(j, carry):
             lanes = lane_block(j)
@@ -291,38 +361,26 @@
             if pair[1] in [c for _, c in onward]:
                 to_left(hop + 1, pair[1]).start()
         if hop == 1:
-            part[1] = sum_part(0)
-            send_part(1)
-        if hop == 2:
-            part[2] = sum_part(1)
-            send_part(2)
-        if hop == 3:
-            total = sum_part(2)
-            rigid = jnp.concatenate([stiff[...], stiff[...]], axis=1)
-            amp = total / rigid
-            both = jnp.concatenate([jnp.where(first_half, amp, 0.0), jnp.where(first_half, 0.0, amp)], axis=0)
-            moved = dot(both, phi[...], ((1,), (0,)))
-            spread = []
-            for i in range(HELD):
-                disp = jnp.sum(jnp.where(picks[i], moved, 0.0), axis=0, keepdims=True)
-                spread.append(jnp.where(at_low, disp, 0.0))
-            dsc[...] = dot(at_high, jnp.concatenate(spread, axis=0), ((1,), (1,)))
-
-            def wall(j, carry):
-                lanes = lane_block(j)
-                for i in range(HELD):
-                    field = dsc[pl.ds(pl.multiple_of(j * CX, CX), CX), pl.ds(i * LANES, LANES)]
-                    for k in range(COMP):
-                        at = pl.ds((i * COMP + k) * CX, CX)
-                        out[at, lanes] = out[at, lanes] + cpl[k] * field
-                return carry
-
-            lax.fori_loop(0, NB_LANE, wall, 0)
+            lax.fori_loop(0, NB_LANE, local, 0)
         if hop < half:
             add_blocks([(fromleft.at[hop - 1], hop), (fromright.at[hop - 1], -hop)], 0, NB_LANE)
         else:
             add_blocks([(fromleft.at[hop - 1], hop)], 0, NB_LANE // 2)
             add_blocks([(fromright.at[hop - 1], -hop)], NB_LANE // 2, NB_LANE)
+
+    total = sum_part(1)
+    rigid = jnp.concatenate([stiff[...], stiff[...]], axis=1)
+    amp = total / rigid
+    both = jnp.concatenate([jnp.where(first_half, amp, 0.0), jnp.where(first_half, 0.0, amp)], axis=0)
+    moved = dot(both, phi[...], ((1,), (0,)))
+    spread = []
+    for i in range(HELD):
+        disp = jnp.sum(jnp.where(picks[i], moved, 0.0), axis=0, keepdims=True)
+        spread.append(jnp.where(at_low, disp, 0.0))
+    hit = dot(at_high, jnp.concatenate(spread, axis=0), ((1,), (1,)))
+    for i in range(HELD):
+        for j in range(NB_LANE):
+            field[pl.ds(i * CX, CX), pl.ds(j * LANES, LANES)] = hit[j * CX : (j + 1) * CX, i * LANES : (i + 1) * LANES]
 
     for hop in range(1, half + 1):
         for c_right, c_left in going(hop):
@@ -330,53 +388,18 @@
             to_left(hop, c_left).wait_send()
     for copy in halos:
         copy.wait_send()
-    for s in range(3):
-        box = stages[s][3]
-        pltpu.make_async_copy(box, box, as_sem.at[s]).wait()
+    for s in range(2):
+        pltpu.make_async_copy(boxes[s], boxes[s], as_sem.at[s]).wait()
 
 
 def body(sizes, state, fx, fc, pw, cpl, modes, stiff, index, count, owner, shift):
     n_space, n_inst, n_blade = sizes
     half = n_inst // 2
-    smem = pl.BlockSpec(memory_space=pltpu.SMEM)
+    stages = exchange_stages(sizes)
     vmem = pl.BlockSpec(memory_space=pltpu.VMEM)
-    hbm = pl.BlockSpec(memory_space=pl.ANY)
+    hbm = pl.BlockSpec(memory_space=pltpu.HBM)
     dma = pltpu.SemaphoreType.DMA
-    out = pl.pallas_call(
-        functools.partial(kernel, sizes),
-        out_shape=jax.ShapeDtypeStruct((DEEP, NC), F32),
-        in_specs=[hbm, smem, smem, smem, smem, hbm, vmem, vmem, smem, vmem, smem],
-        out_specs=vmem,
-        scratch_shapes=[
-            pltpu.VMEM((DEEP, NC), jnp.bfloat16),
-            pltpu.VMEM((2 * MODES, ROWS), F32),
-            pltpu.VMEM((DEEP, NC), F32),
-            pltpu.VMEM((half, DEEP, NC), jnp.bfloat16),
-            pltpu.VMEM((half, DEEP, NC), jnp.bfloat16),
-            pltpu.VMEM((2, 16, NC), F32),
-            pltpu.VMEM((2, 16, NC), jnp.bfloat16),
-            pltpu.VMEM((2, 16, NC), jnp.bfloat16),
-            pltpu.VMEM((CX * NB_LANE, HELD * LANES), F32),
-            pltpu.VMEM((CX * NB_LANE, HELD * LANES), F32),
-            pltpu.VMEM((3, CX, LANES), F32),
-            pltpu.VMEM((n_space - 1, CX, LANES), F32),
-            pltpu.VMEM((n_blade - 1, CX, LANES), F32),
-            pltpu.VMEM((n_inst - 1, CX, LANES), F32),
-            dma((3,)),
-            dma((half, CHUNKS)),
-            dma((half, CHUNKS)),
-            dma((half, CHUNKS)),
-            dma((half, CHUNKS)),
-            dma((2,)),
-            dma((2,)),
-            dma((3,)),
-            dma((3,)),
-        ],
-        compiler_params=pltpu.CompilerParams(
-            collective_id=0, has_side_effects=True, vmem_limit_bytes=24 * 1024 * 1024
-        ),
-        name="residual",
-    )(
+    operands = (
         state.reshape(DEEP, NC),
         fx,
         fc,
@@ -385,11 +408,51 @@
         modes.reshape(MODES, ROWS),
         stiff.reshape(1, MODES),
         index,
-        count,
         owner,
         shift,
     )
-    return out.reshape(1, HELD, COMP, CX, NC)
+    out, field, gain = pl.pallas_call(
+        functools.partial(kernel, sizes),
+        out_shape=(jax.ShapeDtypeStruct((DEEP, NC), F32), jax.ShapeDtypeStruct((HELD * CX, NC), F32), jax.ShapeDtypeStruct((COMP,), F32)),
+        in_specs=[pl.BlockSpec(memory_space=pltpu.SMEM)] + [hbm] * len(operands),
+        out_specs=(vmem, vmem, vmem),
+        scratch_shapes=[
+            pltpu.VMEM((DEEP, NC), jnp.bfloat16),
+            pltpu.VMEM((2 * MODES, ROWS), F32),
+            pltpu.SMEM((COMP, COMP), F32),
+            pltpu.SMEM((COMP, COMP), F32),
+            pltpu.SMEM((COMP,), F32),
+            pltpu.VMEM((1, MODES), F32),
+            pltpu.VMEM((1, ROWS), jnp.int32),
+            pltpu.VMEM((1, ROWS), jnp.int32),
+            pltpu.SMEM((n_blade * BPG,), jnp.int32),
+            pltpu.VMEM((DEEP, NC), F32),
+            pltpu.VMEM((half, DEEP, NC), jnp.bfloat16),
+            pltpu.VMEM((half, DEEP, NC), jnp.bfloat16),
+            pltpu.VMEM((2, 16, NC), F32),
+            pltpu.VMEM((2, 16, NC), jnp.bfloat16),
+            pltpu.VMEM((2, 16, NC), jnp.bfloat16),
+            pltpu.VMEM((CX * NB_LANE, HELD * LANES), F32),
+            pltpu.VMEM((2, CX, LANES), F32),
+            pltpu.VMEM((len(stages[0]), CX, LANES), F32),
+            pltpu.VMEM((len(stages[1]), CX, LANES), F32),
+            dma((len(operands) + 1,)),
+            dma((half, CHUNKS)),
+            dma((half, CHUNKS)),
+            dma((half, CHUNKS)),
+            dma((half, CHUNKS)),
+            dma((2,)),
+            dma((2,)),
+            dma((2,)),
+            dma((2,)),
+        ],
+        compiler_params=pltpu.CompilerParams(
+            collective_id=0, has_side_effects=True, vmem_limit_bytes=24 * 1024 * 1024
+        ),
+        name="residual",
+    )(count, *[pltpu.with_memory_space_constraint(operand, pltpu.HBM) for operand in operands])
+    wall = gain[None, :, None, None] * field.reshape(HELD, 1, CX, NC)
+    return (out.reshape(HELD, COMP, CX, NC) + wall)[None]
 
 
 def solution(mesh):

time: 45.5 us -> 39.7 us (0.87)
  the two profiles are of different devices: /device:TPU:1 before, /device:TPU:8 now
where the time goes in v2:
time: 39.7 us; the launch traced here: 39.5 us
  Pallas kernels  38 us (96%)
  other arithmetic  0.82 us (2%)
  between operations  0.66 us (2%)
    pallas_call x1, Pallas kernels, body(): pl.pallas_call(functools.partial(kernel, sizes), out_shape=(jax.ShapeDtyp...  38 us
    add x1, other arithmetic, body(): return (out.reshape(HELD, COMP, CX, NC) + wall)[None]  0.82 us

profile of v2, /device:TPU:8, one launch (start us, length us, event | category | flops | bytes accessed | tf_op | source)
XLA Modules:
  0.0 39.5 jit_solution(8564924356160274101)
XLA Ops:
  0.7 38.0 %residual.1 = (f32[80,1024]{1,0:T(8,128)S(1)}, f32[16,1024]{1,0:T(8,128)S(1)}, f32[5]{0:T(128)S(1)}) custom-call(s32[1,1]{1,0:T(1,128)S(6)} %copy.12.count, bf16[80,1024]{1,0:T(8,128)(2,1)} %bitcast.7, f32[5,5]{1,0:T(8,128)} %fx_hbm.1, f32[5,5]{1,0:T(8,128)} %fc_hbm.1, f32[5]{0:T(128)} %pw_hbm.1, f32[5]{0:T(128)} %cpl_hbm.1, f32[64,256]{1,0:T(8,128)} %bitcast.8, ...), custom_call_target="tpu_custom_call" | custom-call | tf_op jit(solution)/shard_map/residual/pallas_call | solution.py:414
  38.7 0.8 %multiply_add_fusion = f32[1,2,5,8,1024]{4,3,2,1,0:T(8,128)} fusion(f32[1,2,5,8,1024]{4,3,2,1,0:T(8,128)S(1)} %bitcast.5, f32[2,8,1024]{2,1,0:T(8,128)S(1)} %bitcast.6, f32[5]{0:T(128)S(1)} %get-tuple-element.9), kind=kLoop, calls=%fused_computation | loop fusion | flops 163840 | bytes 720916 | tf_op jit(solution)/shard_map/add | solution.py:455

commit v3 on v2

--- a/solution.py
+++ b/solution.py
@@ -22,10 +22,11 @@
 NB_LANE = NC // LANES
 CHUNKS = 4
 WIDTH = NC // CHUNKS
-STAGES = (("x", "y"), ("zhi", "zlo", "core"))
+
 
 HIGH = lax.Precision.HIGHEST
 MESH = pl.DeviceIdType.MESH
+LOGICAL = pl.DeviceIdType.LOGICAL
 F32 = jnp.float32
 
 
@@ -44,39 +45,36 @@
 SUB = {"zhi": 3, "x": 4, "y": 8, "zlo": 4, "core": 2}
 
 
-def sub_index(at):
-    return {
-        "zhi": at["space"] // SUB["x"],
-        "x": lax.rem(at["space"], SUB["x"]),
-        "y": at["inst"],
-        "zlo": at["blade"] // SUB["core"],
-        "core": lax.rem(at["blade"], SUB["core"]),
+STEP = {"core": 1, "zlo": 2, "y": 8, "x": 64, "zhi": 256}
+
+
+def around(offset, size):
+    return min(offset, size - offset)
+
+
+LINE = list(itertools.product(range(SUB["zlo"]), range(SUB["core"])))
+PLANE = sorted(
+    (o for o in itertools.product(range(SUB["x"]), range(SUB["y"])) if any(o)),
+    key=lambda o: -around(o[0], SUB["x"]) - around(o[1], SUB["y"]),
+)
+FOLLOW = SUB["zhi"] - 1
+
+
+def place(space, inst, blade):
+    here = {
+        "zhi": space // SUB["x"],
+        "x": space % SUB["x"],
+        "y": inst,
+        "zlo": blade // SUB["core"],
+        "core": blade % SUB["core"],
     }
-
-
-def mesh_index(sub):
-    return {
-        "space": sub["zhi"] * SUB["x"] + sub["x"],
-        "inst": sub["y"],
-        "blade": sub["zlo"] * SUB["core"] + sub["core"],
-    }
-
-
-def exchange_stages(sizes):
-    assert sizes == (SUB["zhi"] * SUB["x"], SUB["y"], SUB["zlo"] * SUB["core"])
-
-    def around(offset, size):
-        return min(offset, size - offset)
-
-    def hops(o):
-        return around(o["x"], 4) + around(o["y"], 8) + around((4 * o["zhi"] + o["zlo"]) % 12, 12) + 0.5 * o["core"]
-
-    stages = []
-    for axes in STAGES:
-        ranges = [range(SUB[a]) if a in axes else (0,) for a in SUB]
-        offsets = [dict(zip(SUB, o)) for o in itertools.product(*ranges) if any(o)]
-        stages.append(sorted(offsets, key=lambda o: -hops(o)))
-    return stages
+    table = {}
+    for axis, size in SUB.items():
+        table[axis] = []
+        for offset in range(size):
+            at = here[axis] + offset
+            table[axis].append(jnp.where(at >= size, at - size, at) * STEP[axis])
+    return here, table
 
 
 def kernel(
@@ -114,6 +112,7 @@
     part,
     box0,
     box1,
+    whole,
     load_sem,
     sl_sem,
     rl_sem,
@@ -148,12 +147,16 @@
     for copy in loads:
         copy.start()
 
-    stages = exchange_stages(sizes)
-    mesh_at = {"space": my_space, "inst": my_inst, "blade": my_blade}
-    my_sub = sub_index(mesh_at)
-
-    def peer(offsets):
-        return mesh_index({a: lax.rem(my_sub[a] + offsets[a], SUB[a]) if offsets[a] else my_sub[a] for a in SUB})
+    here, table = place(my_space, my_inst, my_blade)
+    column = table["x"][0] + table["y"][0]
+    stack = table["zlo"][0] + table["core"][0]
+    collects = here["zhi"] == 0
+
+    def on_line(zhi, offsets):
+        return column + zhi * STEP["zhi"] + table["zlo"][offsets[0]] + table["core"][offsets[1]]
+
+    def on_plane(offsets):
+        return stack + table["x"][offsets[0]] + table["y"][offsets[1]]
 
     right = lax.rem(my_inst + 1, n_inst)
     left = lax.rem(my_inst + n_inst - 1, n_inst)
@@ -161,10 +164,32 @@
     preceding = lax.rem(my_space + n_space - 1, n_space)
 
     barrier = pltpu.get_barrier_semaphore()
-    greeted = [peer(o) for stage in stages for o in stage]
-    greeted += [{"space": following}, {"space": preceding}]
-    for other in greeted:
-        pl.semaphore_signal(barrier, inc=1, device_id=other, device_id_type=MESH)
+
+    def greet(other):
+        pl.semaphore_signal(barrier, inc=1, device_id=other, device_id_type=LOGICAL)
+
+    first_x, last_x = here["x"] == 0, here["x"] == SUB["x"] - 1
+    first_block, last_block = my_space == 0, my_space == n_space - 1
+    up_step = last_x & (here["zhi"] < FOLLOW)
+
+    def greet_space(other):
+        pl.semaphore_signal(barrier, inc=1, device_id={"space": other}, device_id_type=MESH)
+
+    for other in (left, right):
+        pl.semaphore_signal(barrier, inc=1, device_id={"inst": other}, device_id_type=MESH)
+    pl.when(jnp.logical_not(first_x))(lambda: greet_space(preceding))
+    pl.when(jnp.logical_not(last_block))(lambda: greet_space(following))
+    sides = jnp.where(first_block | last_x, 1, 2)
+
+    @pl.when(collects)
+    def _():
+        for offsets in reversed(PLANE):
+            greet(on_plane(offsets))
+        for offsets in LINE[1:]:
+            greet(on_line(0, offsets))
+        for zhi in range(1, FOLLOW + 1):
+            for offsets in LINE:
+                greet(on_line(zhi, offsets))
 
     def columns(chunk):
         return pl.ds(chunk * WIDTH, WIDTH)
@@ -241,29 +266,38 @@
     first_half = lax.broadcasted_iota(jnp.int32, (CX, LANES), 1) < MODES
     part[0] = jnp.where(first_half, force[0:CX], force[CX : 2 * CX])
 
-    boxes = (box0, box1)
-
-    def send_part(s):
-        for k, offsets in enumerate(stages[s]):
-            pltpu.make_async_remote_copy(
-                src_ref=part.at[s],
-                dst_ref=boxes[s].at[k],
-                send_sem=as_sem.at[s],
-                recv_sem=ar_sem.at[s],
-                device_id=peer(offsets),
-                device_id_type=MESH,
-            ).start()
-
-    def sum_part(s):
-        box = boxes[s]
-        pltpu.make_async_copy(box, box, ar_sem.at[s]).wait()
-        total = part[s]
-        for k in range(len(stages[s])):
+    def tile(src, dst, stage, other):
+        return pltpu.make_async_remote_copy(
+            src_ref=src,
+            dst_ref=dst,
+            send_sem=as_sem.at[stage],
+            recv_sem=ar_sem.at[stage],
+            device_id=other,
+            device_id_type=LOGICAL,
+        )
+
+    def tiles(number, sem):
+        some = box1.at[pl.ds(0, number)]
+        return pltpu.make_async_copy(some, some, sem)
+
+    def sum_box(first, box, number, stage):
+        pltpu.make_async_copy(box, box, ar_sem.at[stage]).wait()
+        total = first
+        for k in range(number):
             total = total + box[k]
         return total
 
-    pl.semaphore_wait(barrier, len(greeted))
-    send_part(0)
+    @pl.when(collects)
+    def _():
+        pl.semaphore_wait(barrier, 2 + len(PLANE) + len(LINE) - 1 + sides)
+        for k, offsets in enumerate(LINE[1:]):
+            tile(part.at[0], box0.at[FOLLOW * len(LINE) + k], 0, on_line(0, offsets)).start()
+
+    @pl.when(jnp.logical_not(collects))
+    def _():
+        pl.semaphore_wait(barrier, 2 + len(LINE) + sides)
+        for k, offsets in enumerate(LINE):
+            tile(part.at[0], box0.at[(here["zhi"] - 1) * len(LINE) + k], 0, on_line(0, offsets)).start()
 
     for c_right, c_left in going(1):
         to_right(1, c_right).start()
@@ -290,7 +324,9 @@
                 device_id_type=MESH,
             )
         )
-        halos[-1].start()
+
+    pl.when(jnp.logical_not(first_block))(halos[0].start)
+    pl.when(jnp.logical_not(last_block | up_step))(halos[1].start)
 
     for group in range(DEEP // 16):
         pair = mine[pl.ds(16 * group, 16), :].astype(F32)
@@ -299,15 +335,23 @@
         dcs[pl.ds(16 * group, 16), :] = ahead - behind
         out[pl.ds(16 * group, 16), :] = pair - 0.25 * (ahead + behind)
 
-    part[1] = sum_part(0)
-    send_part(1)
-
-    for copy in loads[7:]:
-        copy.wait()
-    for copy in halos:
-        copy.wait_recv()
-    hrow[0] = hrecv[0].astype(F32) * jnp.where(my_space == n_space - 1, 0.0, 1.0)
-    hrow[1] = hrecv[1].astype(F32) * jnp.where(my_space == 0, 0.0, 1.0)
+    def receive(hop):
+        onward = going(hop + 1) if hop < half else []
+        for pair in going(hop):
+            to_right(hop, pair[0]).wait_recv()
+            if pair[0] in [c for c, _ in onward]:
+                to_right(hop + 1, pair[0]).start()
+            to_left(hop, pair[1]).wait_recv()
+            if pair[1] in [c for _, c in onward]:
+                to_left(hop + 1, pair[1]).start()
+
+    receive(1)
+
+    @pl.when(collects)
+    def _():
+        part[1] = sum_box(part[0], box0, (FOLLOW + 1) * len(LINE) - 1, 0)
+        for k, offsets in enumerate(PLANE):
+            tile(part.at[1], box1.at[k], 1, on_plane(offsets)).start()
 
     layer = lax.broadcasted_iota(jnp.int32, (CX, LANES), 0)
 
@@ -351,24 +395,45 @@
 
         lax.fori_loop(first, last, add, 0)
 
-    for hop in range(1, half + 1):
-        onward = going(hop + 1) if hop < half else []
-        for pair in going(hop):
-            to_right(hop, pair[0]).wait_recv()
-            if pair[0] in [c for c, _ in onward]:
-                to_right(hop + 1, pair[0]).start()
-            to_left(hop, pair[1]).wait_recv()
-            if pair[1] in [c for _, c in onward]:
-                to_left(hop + 1, pair[1]).start()
-        if hop == 1:
-            lax.fori_loop(0, NB_LANE, local, 0)
-        if hop < half:
-            add_blocks([(fromleft.at[hop - 1], hop), (fromright.at[hop - 1], -hop)], 0, NB_LANE)
-        else:
-            add_blocks([(fromleft.at[hop - 1], hop)], 0, NB_LANE // 2)
-            add_blocks([(fromright.at[hop - 1], -hop)], NB_LANE // 2, NB_LANE)
-
-    total = sum_part(1)
+    for hop in range(1, half):
+        if hop > 1:
+            receive(hop)
+        add_blocks([(fromleft.at[hop - 1], hop), (fromright.at[hop - 1], -hop)], 0, NB_LANE)
+
+    for copy in loads[7:]:
+        copy.wait()
+    pl.when(jnp.logical_not(last_block))(halos[0].wait_recv)
+    pl.when(up_step)(halos[1].start)
+    pl.when(jnp.logical_not(first_block))(halos[1].wait_recv)
+
+    def neighbour(side, end):
+        @pl.when(end)
+        def _():
+            hrow[side] = jnp.zeros((16, NC), F32)
+
+        @pl.when(jnp.logical_not(end))
+        def _():
+            hrow[side] = hrecv[side].astype(F32)
+
+    neighbour(0, last_block)
+    neighbour(1, first_block)
+    lax.fori_loop(0, NB_LANE, local, 0)
+
+    @pl.when(collects)
+    def _():
+        whole[...] = sum_box(part[1], box1, len(PLANE), 1)
+        for zhi in range(1, FOLLOW + 1):
+            tile(whole, whole, 2, on_line(zhi, LINE[0])).start()
+
+    receive(half)
+    add_blocks([(fromleft.at[half - 1], half)], 0, NB_LANE // 2)
+    add_blocks([(fromright.at[half - 1], -half)], NB_LANE // 2, NB_LANE)
+
+    @pl.when(jnp.logical_not(collects))
+    def _():
+        pltpu.make_async_copy(whole, whole, ar_sem.at[2]).wait()
+
+    total = whole[...]
     rigid = jnp.concatenate([stiff[...], stiff[...]], axis=1)
     amp = total / rigid
     both = jnp.concatenate([jnp.where(first_half, amp, 0.0), jnp.where(first_half, 0.0, amp)], axis=0)
@@ -386,16 +451,24 @@
         for c_right, c_left in going(hop):
             to_right(hop, c_right).wait_send()
             to_left(hop, c_left).wait_send()
-    for copy in halos:
-        copy.wait_send()
-    for s in range(2):
-        pltpu.make_async_copy(boxes[s], boxes[s], as_sem.at[s]).wait()
+    pl.when(jnp.logical_not(first_block))(halos[0].wait_send)
+    pl.when(jnp.logical_not(last_block))(halos[1].wait_send)
+
+    @pl.when(collects)
+    def _():
+        tiles(len(LINE) - 1, as_sem.at[0]).wait()
+        tiles(len(PLANE), as_sem.at[1]).wait()
+        tiles(FOLLOW, as_sem.at[2]).wait()
+
+    @pl.when(jnp.logical_not(collects))
+    def _():
+        tiles(len(LINE), as_sem.at[0]).wait()
 
 
 def body(sizes, state, fx, fc, pw, cpl, modes, stiff, index, count, owner, shift):
     n_space, n_inst, n_blade = sizes
     half = n_inst // 2
-    stages = exchange_stages(sizes)
+    assert sizes == (SUB["zhi"] * SUB["x"], SUB["y"], SUB["zlo"] * SUB["core"])
     vmem = pl.BlockSpec(memory_space=pltpu.VMEM)
     hbm = pl.BlockSpec(memory_space=pltpu.HBM)
     dma = pltpu.SemaphoreType.DMA
@@ -434,8 +507,9 @@
             pltpu.VMEM((2, 16, NC), jnp.bfloat16),
             pltpu.VMEM((CX * NB_LANE, HELD * LANES), F32),
             pltpu.VMEM((2, CX, LANES), F32),
-            pltpu.VMEM((len(stages[0]), CX, LANES), F32),
-            pltpu.VMEM((len(stages[1]), CX, LANES), F32),
+            pltpu.VMEM(((FOLLOW + 1) * len(LINE) - 1, CX, LANES), F32),
+            pltpu.VMEM((len(PLANE), CX, LANES), F32),
+            pltpu.VMEM((CX, LANES), F32),
             dma((len(operands) + 1,)),
             dma((half, CHUNKS)),
             dma((half, CHUNKS)),
@@ -443,8 +517,8 @@
             dma((half, CHUNKS)),
             dma((2,)),
             dma((2,)),
-            dma((2,)),
-            dma((2,)),
+            dma((3,)),
+            dma((3,)),
         ],
         compiler_params=pltpu.CompilerParams(
             collective_id=0, has_side_effects=True, vmem_limit_bytes=24 * 1024 * 1024

time: 39.7 us -> 35.2 us (0.89)
  the two profiles are of different devices: /device:TPU:8 before, /device:TPU:1 now
where the time goes in v3:
time: 35.2 us; the launch traced here: 35 us
  Pallas kernels  33.5 us (95%)
  other arithmetic  0.82 us (2%)
  between operations  0.66 us (2%)
    pallas_call x1, Pallas kernels, body(): pl.pallas_call(functools.partial(kernel, sizes), out_shape=(jax.ShapeDtyp...  33.5 us
    add x1, other arithmetic, body(): return (out.reshape(HELD, COMP, CX, NC) + wall)[None]  0.82 us

profile of v3, /device:TPU:1, one launch (start us, length us, event | category | flops | bytes accessed | tf_op | source)
XLA Modules:
  0.0 35.0 jit_solution(17566899692685175395)
XLA Ops:
  0.7 33.5 %residual.1 = (f32[80,1024]{1,0:T(8,128)S(1)}, f32[16,1024]{1,0:T(8,128)S(1)}, f32[5]{0:T(128)S(1)}) custom-call(s32[1,1]{1,0:T(1,128)S(6)} %copy.12.count, bf16[80,1024]{1,0:T(8,128)(2,1)} %bitcast.7, f32[5,5]{1,0:T(8,128)} %fx_hbm.1, f32[5,5]{1,0:T(8,128)} %fc_hbm.1, f32[5]{0:T(128)} %pw_hbm.1, f32[5]{0:T(128)} %cpl_hbm.1, f32[64,256]{1,0:T(8,128)} %bitcast.8, ...), custom_call_target="tpu_custom_call" | custom-call | tf_op jit(solution)/shard_map/residual/pallas_call | solution.py:487
  34.2 0.8 %multiply_add_fusion = f32[1,2,5,8,1024]{4,3,2,1,0:T(8,128)} fusion(f32[1,2,5,8,1024]{4,3,2,1,0:T(8,128)S(1)} %bitcast.5, f32[2,8,1024]{2,1,0:T(8,128)S(1)} %bitcast.6, f32[5]{0:T(128)S(1)} %get-tuple-element.9), kind=kLoop, calls=%fused_computation | loop fusion | flops 163840 | bytes 720916 | tf_op jit(solution)/shard_map/add | solution.py:529

commit v4 on v3

--- a/solution.py
+++ b/solution.py
@@ -22,6 +22,7 @@
 NB_LANE = NC // LANES
 CHUNKS = 4
 WIDTH = NC // CHUNKS
+EARLY = 3
 
 
 HIGH = lax.Precision.HIGHEST
@@ -335,9 +336,9 @@
         dcs[pl.ds(16 * group, 16), :] = ahead - behind
         out[pl.ds(16 * group, 16), :] = pair - 0.25 * (ahead + behind)
 
-    def receive(hop):
+    def receive(hop, first=0, last=None):
         onward = going(hop + 1) if hop < half else []
-        for pair in going(hop):
+        for pair in going(hop)[first:last]:
             to_right(hop, pair[0]).wait_recv()
             if pair[0] in [c for c, _ in onward]:
                 to_right(hop + 1, pair[0]).start()
@@ -346,6 +347,13 @@
                 to_left(hop + 1, pair[1]).start()
 
     receive(1)
+
+    @pl.when(up_step)
+    def _():
+        halos[0].wait_recv()
+        halos[1].start()
+
+    receive(2, 0, EARLY)
 
     @pl.when(collects)
     def _():
@@ -397,13 +405,12 @@
 
     for hop in range(1, half):
         if hop > 1:
-            receive(hop)
+            receive(hop, EARLY if hop == 2 else 0)
         add_blocks([(fromleft.at[hop - 1], hop), (fromright.at[hop - 1], -hop)], 0, NB_LANE)
 
     for copy in loads[7:]:
         copy.wait()
-    pl.when(jnp.logical_not(last_block))(halos[0].wait_recv)
-    pl.when(up_step)(halos[1].start)
+    pl.when(jnp.logical_not(last_block | up_step))(halos[0].wait_recv)
     pl.when(jnp.logical_not(first_block))(halos[1].wait_recv)
 
     def neighbour(side, end):
@@ -419,15 +426,15 @@
     neighbour(1, first_block)
     lax.fori_loop(0, NB_LANE, local, 0)
 
+    receive(half)
+    add_blocks([(fromleft.at[half - 1], half)], 0, NB_LANE // 2)
+    add_blocks([(fromright.at[half - 1], -half)], NB_LANE // 2, NB_LANE)
+
     @pl.when(collects)
     def _():
         whole[...] = sum_box(part[1], box1, len(PLANE), 1)
         for zhi in range(1, FOLLOW + 1):
             tile(whole, whole, 2, on_line(zhi, LINE[0])).start()
-
-    receive(half)
-    add_blocks([(fromleft.at[half - 1], half)], 0, NB_LANE // 2)
-    add_blocks([(fromright.at[half - 1], -half)], NB_LANE // 2, NB_LANE)
 
     @pl.when(jnp.logical_not(collects))
     def _():

time: 35.2 us -> 33.4 us (0.949)
  Pallas kernels: 33.5 us -> 31.6 us
    pallas_call x1, Pallas kernels: 33.5 us -> 31.6 us  [body(): pl.pallas_call(functools.partial(kernel, sizes), out_shape=(jax.ShapeDtyp...]
where the time goes in v4:
time: 33.4 us; the launch traced here: 33.1 us
  Pallas kernels  31.6 us (95%)
  other arithmetic  0.82 us (2%)
  between operations  0.66 us (2%)
    pallas_call x1, Pallas kernels, body(): pl.pallas_call(functools.partial(kernel, sizes), out_shape=(jax.ShapeDtyp...  31.6 us
    add x1, other arithmetic, body(): return (out.reshape(HELD, COMP, CX, NC) + wall)[None]  0.82 us

profile of v4, /device:TPU:1, one launch (start us, length us, event | category | flops | bytes accessed | tf_op | source)
XLA Modules:
  0.0 33.1 jit_solution(6799869841094760520)
XLA Ops:
  0.7 31.6 %residual.1 = (f32[80,1024]{1,0:T(8,128)S(1)}, f32[16,1024]{1,0:T(8,128)S(1)}, f32[5]{0:T(128)S(1)}) custom-call(s32[1,1]{1,0:T(1,128)S(6)} %copy.12.count, bf16[80,1024]{1,0:T(8,128)(2,1)} %bitcast.7, f32[5,5]{1,0:T(8,128)} %fx_hbm.1, f32[5,5]{1,0:T(8,128)} %fc_hbm.1, f32[5]{0:T(128)} %pw_hbm.1, f32[5]{0:T(128)} %cpl_hbm.1, f32[64,256]{1,0:T(8,128)} %bitcast.8, ...), custom_call_target="tpu_custom_call" | custom-call | tf_op jit(solution)/shard_map/residual/pallas_call | solution.py:494
  32.2 0.8 %multiply_add_fusion = f32[1,2,5,8,1024]{4,3,2,1,0:T(8,128)} fusion(f32[1,2,5,8,1024]{4,3,2,1,0:T(8,128)S(1)} %bitcast.5, f32[2,8,1024]{2,1,0:T(8,128)S(1)} %bitcast.6, f32[5]{0:T(128)S(1)} %get-tuple-element.9), kind=kLoop, calls=%fused_computation | loop fusion | flops 163840 | bytes 720916 | tf_op jit(solution)/shard_map/add | solution.py:536

commit v5 on v4

--- a/solution.py
+++ b/solution.py
@@ -76,6 +76,11 @@
             at = here[axis] + offset
             table[axis].append(jnp.where(at >= size, at - size, at) * STEP[axis])
     return here, table
+
+
+def parts(values):
+    upper = values.astype(jnp.bfloat16)
+    return upper, (values - upper.astype(F32)).astype(jnp.bfloat16)
 
 
 def kernel(
@@ -103,6 +108,8 @@
     index,
     owner,
     shift,
+    phis,
+    low_rows,
     dcs,
     fromleft,
     fromright,
@@ -184,7 +191,7 @@
 
     @pl.when(collects)
     def _():
-        for offsets in reversed(PLANE):
+        for offsets in PLANE:
             greet(on_plane(offsets))
         for offsets in LINE[1:]:
             greet(on_line(0, offsets))
@@ -328,6 +335,11 @@
 
     pl.when(jnp.logical_not(first_block))(halos[0].start)
     pl.when(jnp.logical_not(last_block | up_step))(halos[1].start)
+
+    upper, lower = parts(phi[...])
+    for n, term in enumerate((upper, upper, lower)):
+        phis[pl.ds(2 * MODES * n, 2 * MODES), :] = term
+    low_rows[...] = jnp.where(at_low, 1.0, 0.0).T.astype(jnp.bfloat16)
 
     for group in range(DEEP // 16):
         pair = mine[pl.ds(16 * group, 16), :].astype(F32)
@@ -426,15 +438,15 @@
     neighbour(1, first_block)
     lax.fori_loop(0, NB_LANE, local, 0)
 
+    @pl.when(collects)
+    def _():
+        whole[...] = sum_box(part[1], box1, len(PLANE), 1)
+        for zhi in range(1, FOLLOW + 1):
+            tile(whole, whole, 2, on_line(zhi, LINE[0])).start()
+
     receive(half)
     add_blocks([(fromleft.at[half - 1], half)], 0, NB_LANE // 2)
     add_blocks([(fromright.at[half - 1], -half)], NB_LANE // 2, NB_LANE)
-
-    @pl.when(collects)
-    def _():
-        whole[...] = sum_box(part[1], box1, len(PLANE), 1)
-        for zhi in range(1, FOLLOW + 1):
-            tile(whole, whole, 2, on_line(zhi, LINE[0])).start()
 
     @pl.when(jnp.logical_not(collects))
     def _():
@@ -444,15 +456,19 @@
     rigid = jnp.concatenate([stiff[...], stiff[...]], axis=1)
     amp = total / rigid
     both = jnp.concatenate([jnp.where(first_half, amp, 0.0), jnp.where(first_half, 0.0, amp)], axis=0)
-    moved = dot(both, phi[...], ((1,), (0,)))
+    upper, lower = parts(both)
+    moved = jnp.dot(jnp.concatenate([upper, lower, upper], axis=1), phis[...], preferred_element_type=F32)
     spread = []
     for i in range(HELD):
         disp = jnp.sum(jnp.where(picks[i], moved, 0.0), axis=0, keepdims=True)
-        spread.append(jnp.where(at_low, disp, 0.0))
-    hit = dot(at_high, jnp.concatenate(spread, axis=0), ((1,), (1,)))
+        spread.append(at_high * disp)
+    upper, lower = parts(jnp.concatenate(spread, axis=0))
+    hits = [jnp.dot(term, low_rows[...], preferred_element_type=F32) for term in (upper, lower)]
+    hit = hits[0] + hits[1]
     for i in range(HELD):
         for j in range(NB_LANE):
-            field[pl.ds(i * CX, CX), pl.ds(j * LANES, LANES)] = hit[j * CX : (j + 1) * CX, i * LANES : (i + 1) * LANES]
+            at = (i * NB_LANE + j) * CX
+            field[pl.ds(i * CX, CX), pl.ds(j * LANES, LANES)] = hit[at : at + CX]
 
     for hop in range(1, half + 1):
         for c_right, c_left in going(hop):
@@ -506,6 +522,8 @@
             pltpu.VMEM((1, ROWS), jnp.int32),
             pltpu.VMEM((1, ROWS), jnp.int32),
             pltpu.SMEM((n_blade * BPG,), jnp.int32),
+            pltpu.VMEM((6 * MODES, ROWS), jnp.bfloat16),
+            pltpu.VMEM((ROWS, LANES), jnp.bfloat16),
             pltpu.VMEM((DEEP, NC), F32),
             pltpu.VMEM((half, DEEP, NC), jnp.bfloat16),
             pltpu.VMEM((half, DEEP, NC), jnp.bfloat16),

time: 33.4 us -> 33.1 us (level)
  no operation moved by 1% of the time
where the time goes in v5:
time: 33.1 us; the launch traced here: 32.9 us
  Pallas kernels  31.5 us (95%)
  other arithmetic  0.82 us (2%)
  between operations  0.66 us (2%)
    pallas_call x1, Pallas kernels, body(): pl.pallas_call(functools.partial(kernel, sizes), out_shape=(jax.ShapeDtyp...  31.5 us
    add x1, other arithmetic, body(): return (out.reshape(HELD, COMP, CX, NC) + wall)[None]  0.82 us

profile of v5, /device:TPU:1, one launch (start us, length us, event | category | flops | bytes accessed | tf_op | source)
XLA Modules:
  0.0 32.9 jit_solution(9783442809716268197)
XLA Ops:
  0.7 31.5 %residual.1 = (f32[80,1024]{1,0:T(8,128)S(1)}, f32[16,1024]{1,0:T(8,128)S(1)}, f32[5]{0:T(128)S(1)}) custom-call(s32[1,1]{1,0:T(1,128)S(6)} %copy.12.count, bf16[80,1024]{1,0:T(8,128)(2,1)} %bitcast.7, f32[5,5]{1,0:T(8,128)} %fx_hbm.1, f32[5,5]{1,0:T(8,128)} %fc_hbm.1, f32[5]{0:T(128)} %pw_hbm.1, f32[5]{0:T(128)} %cpl_hbm.1, f32[64,256]{1,0:T(8,128)} %bitcast.8, ...), custom_call_target="tpu_custom_call" | custom-call | tf_op jit(solution)/shard_map/residual/pallas_call | solution.py:510
  32.1 0.8 %multiply_add_fusion = f32[1,2,5,8,1024]{4,3,2,1,0:T(8,128)} fusion(f32[1,2,5,8,1024]{4,3,2,1,0:T(8,128)S(1)} %bitcast.5, f32[2,8,1024]{2,1,0:T(8,128)S(1)} %bitcast.6, f32[5]{0:T(128)S(1)} %get-tuple-element.9), kind=kLoop, calls=%fused_computation | loop fusion | flops 163840 | bytes 720916 | tf_op jit(solution)/shard_map/add | solution.py:554

commit v6 on v5

--- a/solution.py
+++ b/solution.py
@@ -298,8 +298,6 @@
     @pl.when(collects)
     def _():
         pl.semaphore_wait(barrier, 2 + len(PLANE) + len(LINE) - 1 + sides)
-        for k, offsets in enumerate(LINE[1:]):
-            tile(part.at[0], box0.at[FOLLOW * len(LINE) + k], 0, on_line(0, offsets)).start()
 
     @pl.when(jnp.logical_not(collects))
     def _():
@@ -310,6 +308,11 @@
     for c_right, c_left in going(1):
         to_right(1, c_right).start()
         to_left(1, c_left).start()
+
+    @pl.when(collects)
+    def _():
+        for k, offsets in enumerate(LINE[1:]):
+            tile(part.at[0], box0.at[FOLLOW * len(LINE) + k], 0, on_line(0, offsets)).start()
 
     hrow[...] = jnp.zeros_like(hrow)
     for group in range(DEEP // 16):

time: 33.1 us -> 33.1 us (level)
  no operation moved by 1% of the time
where the time goes in v6:
time: 33.1 us; the launch traced here: 32.9 us
  Pallas kernels  31.5 us (95%)
  other arithmetic  0.82 us (2%)
  between operations  0.66 us (2%)
    pallas_call x1, Pallas kernels, body(): pl.pallas_call(functools.partial(kernel, sizes), out_shape=(jax.ShapeDtyp...  31.5 us
    add x1, other arithmetic, body(): return (out.reshape(HELD, COMP, CX, NC) + wall)[None]  0.82 us

profile of v6, /device:TPU:1, one launch (start us, length us, event | category | flops | bytes accessed | tf_op | source)
XLA Modules:
  0.0 32.9 jit_solution(4606619680777640330)
XLA Ops:
  0.7 31.5 %residual.1 = (f32[80,1024]{1,0:T(8,128)S(1)}, f32[16,1024]{1,0:T(8,128)S(1)}, f32[5]{0:T(128)S(1)}) custom-call(s32[1,1]{1,0:T(1,128)S(6)} %copy.12.count, bf16[80,1024]{1,0:T(8,128)(2,1)} %bitcast.7, f32[5,5]{1,0:T(8,128)} %fx_hbm.1, f32[5,5]{1,0:T(8,128)} %fc_hbm.1, f32[5]{0:T(128)} %pw_hbm.1, f32[5]{0:T(128)} %cpl_hbm.1, f32[64,256]{1,0:T(8,128)} %bitcast.8, ...), custom_call_target="tpu_custom_call" | custom-call | tf_op jit(solution)/shard_map/residual/pallas_call | solution.py:513
  32.1 0.8 %multiply_add_fusion = f32[1,2,5,8,1024]{4,3,2,1,0:T(8,128)} fusion(f32[1,2,5,8,1024]{4,3,2,1,0:T(8,128)S(1)} %bitcast.5, f32[2,8,1024]{2,1,0:T(8,128)S(1)} %bitcast.6, f32[5]{0:T(128)S(1)} %get-tuple-element.9), kind=kLoop, calls=%fused_computation | loop fusion | flops 163840 | bytes 720916 | tf_op jit(solution)/shard_map/add | solution.py:557
